TPU v7x, 32 devices: a whole 2x2x4 slice. The times are simulated.
32 devices in a mesh: groups: 2 (over y), pipe: 4 (over z), dp: 4 (over x, core).
Axes of the slice: x: 2, y: 2, z: 4, core: 2. Of those that a mesh axis runs over, the one named last changes fastest.
Arguments:
- section_input: bfloat16 [4, 32, 64, 768], P('pipe', ('groups', 'dp')), parts along dimension 1, may hold values from -6 to 6
- depth_kernel: bfloat16 [4, 49, 768], P('pipe'), may hold values from -0.875 to 0.875
- norm_gain: bfloat16 [4, 768], P('pipe'), may hold values from 0.5 to 1.5
- expand_weight: bfloat16 [4, 768, 3072], P('pipe', 'dp'), may hold values from -0.21875 to 0.21875
- shrink_weight: bfloat16 [4, 3072, 768], P('pipe', 'dp'), may hold values from -0.02734375 to 0.02734375
- response_gain: bfloat16 [4, 3072], P('pipe'), may hold values from -3 to 3
- loss_grad: bfloat16 [32, 64, 768], P(('groups', 'dp')), parts along dimension 0, may hold values from -6 to 6
- plan: int32 [8, 4], P(('groups', 'dp')), parts along dimension 0, may hold values from 0 to 3, each once within a row
Outputs:
- input_grad: bfloat16 [4, 32, 64, 768], P('pipe', ('groups', 'dp')), parts along dimension 1
- kernel_grad: float32 [8, 49, 768], P(('groups', 'pipe'), None, 'dp'), parts along dimension 0
- response_grad: float32 [8, 3072], P(('groups', 'pipe'), 'dp'), parts along dimension 0
There are 2 independent parts, one for each index of `groups`. A program takes and returns all parts, laid end to end along the dimension named above; an argument that names none is the same for every part. Nothing has to cross between parts.
Inputs may be any that keep to these rules, and one draw needn't show every extreme that they name: `plan`: each row holds each of the 4 micro-batch numbers once.
All inputs are finite; a program needn't handle non-finite values.
Results may differ from a plain program's by a relative error of at most 0.011.
Values may be sent and summed in bfloat16 or wider, within the bound.
A program may use at most 128 MiB of HBM per device.

v0:
```python
import jax
import jax.numpy as jnp
from jax import lax
from jax.sharding import PartitionSpec as P

KSIDE = 7
SIDE = 8


inverse_root_two = 0.7071067811865476
inverse_root_tau = 0.3989422804014327


def from_behind(value, axis, steps):
    count = lax.axis_size(axis)
    first, last = (max(0, -steps), min(count, count - steps))
    return lax.ppermute(value, axis, [(source, source + steps) for source in range(first, last)])


def depth_forward(images, kernel):
    margin = KSIDE // 2
    padded = jnp.pad(images, ((0, 0), (margin, margin), (margin, margin), (0, 0)))
    total = jnp.zeros_like(images)
    for row_tap in range(KSIDE):
        for col_tap in range(KSIDE):
            total = (
                total
                + kernel[row_tap * KSIDE + col_tap]
                * padded[:, row_tap : row_tap + SIDE, col_tap : col_tap + SIDE, :]
            )
    return total


def depth_transpose(gradient, kernel):
    margin = KSIDE // 2
    padded = jnp.pad(gradient, ((0, 0), (margin, margin), (margin, margin), (0, 0)))
    total = jnp.zeros_like(gradient)
    for row_tap in range(KSIDE):
        for col_tap in range(KSIDE):
            row_at = KSIDE - 1 - row_tap
            col_at = KSIDE - 1 - col_tap
            total = (
                total
                + kernel[row_tap * KSIDE + col_tap]
                * padded[:, row_at : row_at + SIDE, col_at : col_at + SIDE, :]
            )
    return total


def depth_kernel_terms(gradient, images):
    margin = KSIDE // 2
    padded = jnp.pad(images, ((0, 0), (margin, margin), (margin, margin), (0, 0)))
    pieces = []
    for row_tap in range(KSIDE):
        for col_tap in range(KSIDE):
            pieces.append(
                jnp.sum(
                    gradient * padded[:, row_tap : row_tap + SIDE, col_tap : col_tap + SIDE, :],
                    axis=(0, 1, 2),
                )
            )
    return jnp.stack(pieces)


def block_forward(grid_view, kernel, gain_vec, expand):
    channels = grid_view.shape[-1]
    images = grid_view.astype(jnp.float32)
    mixed = depth_forward(images, kernel)
    flattened = mixed.reshape(-1, channels)
    centre = jnp.mean(flattened, axis=-1, keepdims=True)
    offset = flattened - centre
    spread = lax.rsqrt(jnp.mean(offset * offset, axis=-1, keepdims=True) + 1e-06)
    normed = offset * spread
    scaled = (normed * gain_vec).astype(jnp.bfloat16)
    hidden = jnp.dot(scaled, expand, preferred_element_type=jnp.float32)
    return (normed, spread, hidden)


def block_backward(
    upstream, grid_view, normed, spread, hidden, kernel, gain_vec, resp_gain, expand, shrink
):
    image_count = grid_view.shape[0]
    channels = grid_view.shape[-1]
    units = hidden.shape[-1]
    images = grid_view.astype(jnp.float32)
    back_resp = lax.dot_general(
        upstream, shrink, (((1,), (1,)), ((), ())), preferred_element_type=jnp.float32
    )
    erf_part = 0.5 * (1.0 + lax.erf(hidden * inverse_root_two))
    activation = (hidden * erf_part).reshape(image_count, -1, units)
    back_image = back_resp.reshape(image_count, -1, units)
    energy = jnp.sqrt(jnp.sum(activation * activation, axis=1, keepdims=True) + 1e-06)
    average = jnp.mean(energy, axis=2, keepdims=True) + 1e-06
    norm_ratio = energy / average
    weighted = jnp.sum(back_image * activation, axis=1, keepdims=True) * resp_gain
    back_energy = weighted / average - jnp.sum(weighted * energy, axis=2, keepdims=True) / (
        average * average * units
    )
    back_activ = back_image * (1.0 + resp_gain * norm_ratio) + activation * (back_energy / energy)
    gelu_slope = erf_part + hidden * jnp.exp(-0.5 * hidden * hidden) * inverse_root_tau
    back_hidden = (back_activ.reshape(-1, units) * gelu_slope).astype(jnp.bfloat16)
    back_scaled = lax.dot_general(
        back_hidden, expand, (((1,), (1,)), ((), ())), preferred_element_type=jnp.float32
    )
    scaled_grad = back_scaled * gain_vec
    back_mixed = (
        scaled_grad
        - jnp.mean(scaled_grad, axis=-1, keepdims=True)
        - normed * jnp.mean(scaled_grad * normed, axis=-1, keepdims=True)
    ) * spread
    back_grid = back_mixed.reshape(image_count, SIDE, SIDE, channels)
    branch = depth_transpose(back_grid, kernel).reshape(-1, channels)
    grad_in = (upstream.astype(jnp.float32) + branch).astype(jnp.bfloat16)
    kernel_term = depth_kernel_terms(back_grid, images)
    gain_term = jnp.sum(back_image * activation * norm_ratio, axis=(0, 1))
    return (grad_in, kernel_term, gain_term)


def on_device(
    section_input,
    depth_kernel,
    norm_gain,
    expand_weight,
    shrink_weight,
    response_gain,
    loss_grad,
    plan,
):
    expand_full, shrink_full = (
        lax.all_gather(expand_weight, "dp", axis=1, tiled=True),
        lax.all_gather(shrink_weight, "dp", axis=1, tiled=True),
    )
    expand = expand_full[0]
    shrink = shrink_full[0]
    kernel = depth_kernel[0].astype(jnp.float32)
    gain_vec = norm_gain[0].astype(jnp.float32)
    resp_gain = response_gain[0].astype(jnp.float32)
    local_x = section_input[0]
    micro_count = local_x.shape[0]
    row_count = local_x.shape[1]
    channels = local_x.shape[2]
    units = expand.shape[1]
    sections = lax.axis_size("pipe")
    position = lax.axis_index("pipe")
    step_count = sections + micro_count - 1
    normed_all, spread_all, hidden_all = block_forward(
        local_x.reshape(-1, SIDE, SIDE, channels), kernel, gain_vec, expand
    )
    stored = (
        normed_all.reshape(micro_count, row_count, channels),
        spread_all.reshape(micro_count, row_count, 1),
        hidden_all.reshape(micro_count, row_count, units),
    )

    def run_section(operands):
        upstream, member, result, kern_acc, gain_acc = operands
        images = lax.dynamic_index_in_dim(local_x, member, 0, keepdims=False)
        grid_view = images.reshape(-1, SIDE, SIDE, channels)
        normed = lax.dynamic_index_in_dim(stored[0], member, 0, keepdims=False)
        spread = lax.dynamic_index_in_dim(stored[1], member, 0, keepdims=False)
        hidden = lax.dynamic_index_in_dim(stored[2], member, 0, keepdims=False)
        grad_in, kernel_term, gain_term = block_backward(
            upstream, grid_view, normed, spread, hidden, kernel, gain_vec, resp_gain, expand, shrink
        )
        result = lax.dynamic_update_index_in_dim(result, grad_in, member, 0)
        return (grad_in, result, kern_acc + kernel_term, gain_acc + gain_term)

    def pass_over(operands):
        upstream, member, result, kern_acc, gain_acc = operands
        return (jnp.zeros_like(upstream), result, kern_acc, gain_acc)

    def advance(step_index, state_now):
        incoming, result, kern_acc, gain_acc = state_now
        slot_index = step_index - (sections - 1 - position)
        active = (slot_index >= 0) & (slot_index < micro_count)
        slot_safe = jnp.clip(slot_index, 0, micro_count - 1)
        member = plan[0, slot_safe]
        from_loss = lax.dynamic_index_in_dim(loss_grad, slot_safe, 0, keepdims=False)
        upstream = jnp.where(position == sections - 1, from_loss, incoming)
        outgoing, result, kern_acc, gain_acc = lax.cond(
            active, run_section, pass_over, (upstream, member, result, kern_acc, gain_acc)
        )
        incoming = from_behind(outgoing, "pipe", -1)
        return (incoming, result, kern_acc, gain_acc)

    start_state = (
        jnp.zeros((row_count, channels), jnp.bfloat16),
        jnp.zeros((micro_count, row_count, channels), jnp.bfloat16),
        jnp.zeros((KSIDE * KSIDE, channels), jnp.float32),
        jnp.zeros((units,), jnp.float32),
    )
    leftover, result, kern_acc, gain_acc = lax.fori_loop(0, step_count, advance, start_state)
    kern_share, gain_share = (
        lax.psum_scatter(
            kern_acc[None].astype(jnp.bfloat16), "dp", scatter_dimension=2, tiled=True
        ).astype(jnp.float32),
        lax.psum_scatter(
            gain_acc.reshape(1, 1, units).astype(jnp.bfloat16),
            "dp",
            scatter_dimension=2,
            tiled=True,
        ).astype(jnp.float32),
    )
    return (result[None], kern_share, gain_share.reshape(1, -1))


def solution(mesh):
    placed = (
        P("pipe", ("groups", "dp"), None, None),
        P("pipe", None, None),
        P("pipe", None),
        P("pipe", "dp", None),
        P("pipe", "dp", None),
        P("pipe", None),
        P(("groups", "dp"), None, None),
        P(("groups", "dp"), None),
    )
    return jax.shard_map(
        on_device,
        mesh=mesh,
        in_specs=placed,
        out_specs=(
            P("pipe", ("groups", "dp"), None, None),
            P(("groups", "pipe"), None, "dp"),
            P(("groups", "pipe"), "dp"),
        ),
        check_vma=False,
    )
```

profile of v0, /device:TPU:0, one launch (start us, length us, event | category | flops | bytes accessed | tf_op | source)
XLA Modules:
  0.0 352.7 jit_solution(11973558259606472819)
XLA Ops:
  10.1 1.1 bitcast_convert_fusion
  11.1 5.4 %fusion.283 = (f32[4,8,8]{2,1,0:T(8,128)S(1)}, f32[4,8,8,768]{3,2,1,0:T(8,128)S(1)}) fusion(f32[768]{0:T(1024)S(1)} %get-tuple-element.739, f32[768]{0:T(1024)S(1)} %get-tuple-element.692, f32[768]{0:T(1024)S(1)} %get-tuple-element.693, f32[768]{0:T(1024)S(1)} %get-tuple-element.694, f32[768]{0:T(1024)S(1)} %get-tuple-element.695, ...), kind=kLoop, calls=%fused_computation.554 | loop fusion | flops 19267328 | bytes 1724416 | tf_op jit(solution)/shard_map/reduce_sum | solution.py:70
  17.2 32.5 %all-gather.5.cloned.1.call-done = bf16[1,768,3072]{2,1,0:T(8,128)(2,1)} async-done(((bf16[1,192,3072]{2,1,0:T(8,128)(2,1)}), bf16[1,768,3072]{2,1,0:T(8,128)(2,1)}) %all-gather.5.cloned.1.call-update) | async-done | bytes 4718608 | tf_op jit(solution)/shard_map/all_gather | solution.py:130
  49.8 5.4 %fusion.175 = f32[4,64,3072]{2,1,0:T(8,128)} fusion(bf16[1,768,3072]{2,1,0:T(8,128)(2,1)} %all-gather.5.cloned.1.call-done, f32[4,8,8,768]{3,2,1,0:T(8,128)S(1)} %get-tuple-element.782, f32[768]{0:T(1024)S(1)} %convert_reduce_fusion, f32[4,8,8]{2,1,0:T(8,128)S(1)} %add_rsqrt_fusion, f32[4,8,8]{2,1,0:T(8,128)S(1)} %broadcast_multiply_fusion.2), kind=kOutput, calls=%fused_computation.388 | convolution fusion | flops 1208745984 | bytes 8655872 | tf_op jit(solution)/shard_map/dot_general | solution.py:75
  55.2 33.6 %all-gather.3.cloned.1.call-done = bf16[1,3072,768]{2,1,0:T(8,128)(2,1)} async-done(((bf16[1,768,768]{2,1,0:T(8,128)(2,1)}), bf16[1,3072,768]{2,1,0:T(8,128)(2,1)}) %all-gather.3.cloned.1.call-update) | async-done | bytes 4718608 | tf_op jit(solution)/shard_map/all_gather | solution.py:131
  88.9 176.4 %while.21 = (s32[]{:T(128)}, bf16[64,768]{1,0:T(8,128)(2,1)S(1)}, bf16[4,64,768]{2,1,0:T(8,128)(2,1)S(1)}, f32[49,768]{1,0:T(8,128)S(1)}, f32[3072]{0:T(1024)S(1...) while((s32[]{:T(128)}, bf16[64,768]{1,0:T(8,128)(2,1)S(1)}, ...), condition=%wide.region_61.62_spmd, body=%wide.region_2.61_spmd.sunk | while | flops 619948032 | bytes 28525960 | solution.py:192
  89.0 1.3 collective-permute-start
  90.3 5.5 %collective-permute-done = bf16[64,768]{1,0:T(8,128)(2,1)S(1)} collective-permute-done((bf16[64,768]{1,0:T(8,128)(2,1)S(1)}, bf16[64,768]{1,0:T(8,128)(2,1)S(1)}, u32[]{:S(2)}, u32[]{:S(2)}) %collective-permute-start) | collective-permute-done | bytes 98336 | tf_op jit(solution)/shard_map/while/body/eval_jaxpr/ppermute | solution.py:17
  95.9 1.3 collective-permute-start
  97.2 5.2 %collective-permute-done = bf16[64,768]{1,0:T(8,128)(2,1)S(1)} collective-permute-done((bf16[64,768]{1,0:T(8,128)(2,1)S(1)}, bf16[64,768]{1,0:T(8,128)(2,1)S(1)}, u32[]{:S(2)}, u32[]{:S(2)}) %collective-permute-start) | collective-permute-done | bytes 98336 | tf_op jit(solution)/shard_map/while/body/eval_jaxpr/ppermute | solution.py:17
  102.4 1.3 collective-permute-start
  103.7 60.0 %collective-permute-done = bf16[64,768]{1,0:T(8,128)(2,1)S(1)} collective-permute-done((bf16[64,768]{1,0:T(8,128)(2,1)S(1)}, bf16[64,768]{1,0:T(8,128)(2,1)S(1)}, u32[]{:S(2)}, u32[]{:S(2)}) %collective-permute-start) | collective-permute-done | bytes 98336 | tf_op jit(solution)/shard_map/while/body/eval_jaxpr/ppermute | solution.py:17
  163.7 18.9 %conditional.2 = (bf16[64,768]{1,0:T(8,128)(2,1)S(1)}, bf16[4,64,768]{2,1,0:T(8,128)(2,1)S(1)}, f32[49,768]{1,0:T(8,128)S(1)}, f32[3072]{0:T(1024)S(1)}) conditional(s32[]{:T(128)} %convert_element_type.140, (bf16[4,64,768]{2,1,0:T(8,128)(2,1)S(1)}, f32[49,768]{1,0:T(8,128)S(1)}, f32[3072]{0:T(1024)S(1)}) %tuple.206, (pred[]{:T(512)}, s32[]{:T(128)}, ...), branch_computations={%region_3.3_spmd, %region_4.60_spmd} | conditional | flops 619948032 | bytes 28132316 | solution.py:180
  166.2 1.4 multiply_reduce_fusion.1
  168.9 4.1 %multiply_reduce_fusion = (f32[3072]{0:T(1024)S(1)}, f32[3072]{0:T(1024)S(1)}, f32[64,3072]{1,0:T(8,128)S(1)}) fusion(f32[3072]{0:T(1024)S(1)} %get-tuple-element.780, f32[4,64,3072]{2,1,0:T(8,128)} %get-tuple-element.548, s32[]{:T(128)S(6)} %select_n.44, bf16[3072,768]{1,0:T(8,128)(2,1)} %get-tuple-element.546, ...), kind=kOutput, calls=%fused_computation.61 | convolution fusion | flops 303605760 | bytes 6524937 | tf_op jit(solution)/shard_map/while/body/eval_jaxpr/cond/branch_1_fun/dot_general | solution.py:86
  174.4 4.4 %fusion.279 = (f32[64]{0:T(128)S(1)}, f32[64]{0:T(128)S(1)}, f32[64,768]{1,0:T(8,128)S(1)}) fusion(f32[4,64,768]{2,1,0:T(8,128)S(1)} %get-tuple-element.552, s32[]{:T(128)S(6)} %select_n.44, f32[768]{0:T(1024)S(1)} %get-tuple-element.551, bf16[768,3072]{1,0:T(8,128)(2,1)} %get-tuple-element.550, f32[64,3072]{1,0:T(8,128)S(1)} %get-tuple-element.785, ...), kind=kOutput, calls=%fused_computation.553 | convolution fusion | flops 304938880 | bytes 6713856 | tf_op jit(solution)/shard_map/while/body/eval_jaxpr/cond/branch_1_fun/dot_general | solution.py:102
  181.5 1.1 bitcast_dynamic-update-slice_fusion
  182.6 1.3 collective-permute-start
  183.9 5.2 %collective-permute-done = bf16[64,768]{1,0:T(8,128)(2,1)S(1)} collective-permute-done((bf16[64,768]{1,0:T(8,128)(2,1)S(1)}, bf16[64,768]{1,0:T(8,128)(2,1)S(1)}, u32[]{:S(2)}, u32[]{:S(2)}) %collective-permute-start) | collective-permute-done | bytes 98336 | tf_op jit(solution)/shard_map/while/body/eval_jaxpr/ppermute | solution.py:17
  189.1 18.9 %conditional.2 = (bf16[64,768]{1,0:T(8,128)(2,1)S(1)}, bf16[4,64,768]{2,1,0:T(8,128)(2,1)S(1)}, f32[49,768]{1,0:T(8,128)S(1)}, f32[3072]{0:T(1024)S(1)}) conditional(s32[]{:T(128)} %convert_element_type.140, (bf16[4,64,768]{2,1,0:T(8,128)(2,1)S(1)}, f32[49,768]{1,0:T(8,128)S(1)}, f32[3072]{0:T(1024)S(1)}) %tuple.206, (pred[]{:T(512)}, s32[]{:T(128)}, ...), branch_computations={%region_3.3_spmd, %region_4.60_spmd} | conditional | flops 619948032 | bytes 28132316 | solution.py:180
  191.6 1.4 multiply_reduce_fusion.1
  194.3 4.1 %multiply_reduce_fusion = (f32[3072]{0:T(1024)S(1)}, f32[3072]{0:T(1024)S(1)}, f32[64,3072]{1,0:T(8,128)S(1)}) fusion(f32[3072]{0:T(1024)S(1)} %get-tuple-element.780, f32[4,64,3072]{2,1,0:T(8,128)} %get-tuple-element.548, s32[]{:T(128)S(6)} %select_n.44, bf16[3072,768]{1,0:T(8,128)(2,1)} %get-tuple-element.546, ...), kind=kOutput, calls=%fused_computation.61 | convolution fusion | flops 303605760 | bytes 6524937 | tf_op jit(solution)/shard_map/while/body/eval_jaxpr/cond/branch_1_fun/dot_general | solution.py:86
  199.8 4.4 %fusion.279 = (f32[64]{0:T(128)S(1)}, f32[64]{0:T(128)S(1)}, f32[64,768]{1,0:T(8,128)S(1)}) fusion(f32[4,64,768]{2,1,0:T(8,128)S(1)} %get-tuple-element.552, s32[]{:T(128)S(6)} %select_n.44, f32[768]{0:T(1024)S(1)} %get-tuple-element.551, bf16[768,3072]{1,0:T(8,128)(2,1)} %get-tuple-element.550, f32[64,3072]{1,0:T(8,128)S(1)} %get-tuple-element.785, ...), kind=kOutput, calls=%fused_computation.553 | convolution fusion | flops 304938880 | bytes 6713856 | tf_op jit(solution)/shard_map/while/body/eval_jaxpr/cond/branch_1_fun/dot_general | solution.py:102
  207.0 1.1 bitcast_dynamic-update-slice_fusion
  208.0 1.3 collective-permute-start
  209.3 5.2 %collective-permute-done = bf16[64,768]{1,0:T(8,128)(2,1)S(1)} collective-permute-done((bf16[64,768]{1,0:T(8,128)(2,1)S(1)}, bf16[64,768]{1,0:T(8,128)(2,1)S(1)}, u32[]{:S(2)}, u32[]{:S(2)}) %collective-permute-start) | collective-permute-done | bytes 98336 | tf_op jit(solution)/shard_map/while/body/eval_jaxpr/ppermute | solution.py:17
  214.5 18.9 %conditional.2 = (bf16[64,768]{1,0:T(8,128)(2,1)S(1)}, bf16[4,64,768]{2,1,0:T(8,128)(2,1)S(1)}, f32[49,768]{1,0:T(8,128)S(1)}, f32[3072]{0:T(1024)S(1)}) conditional(s32[]{:T(128)} %convert_element_type.140, (bf16[4,64,768]{2,1,0:T(8,128)(2,1)S(1)}, f32[49,768]{1,0:T(8,128)S(1)}, f32[3072]{0:T(1024)S(1)}) %tuple.206, (pred[]{:T(512)}, s32[]{:T(128)}, ...), branch_computations={%region_3.3_spmd, %region_4.60_spmd} | conditional | flops 619948032 | bytes 28132316 | solution.py:180
  217.0 1.4 multiply_reduce_fusion.1
  219.7 4.1 %multiply_reduce_fusion = (f32[3072]{0:T(1024)S(1)}, f32[3072]{0:T(1024)S(1)}, f32[64,3072]{1,0:T(8,128)S(1)}) fusion(f32[3072]{0:T(1024)S(1)} %get-tuple-element.780, f32[4,64,3072]{2,1,0:T(8,128)} %get-tuple-element.548, s32[]{:T(128)S(6)} %select_n.44, bf16[3072,768]{1,0:T(8,128)(2,1)} %get-tuple-element.546, ...), kind=kOutput, calls=%fused_computation.61 | convolution fusion | flops 303605760 | bytes 6524937 | tf_op jit(solution)/shard_map/while/body/eval_jaxpr/cond/branch_1_fun/dot_general | solution.py:86
  225.2 4.4 %fusion.279 = (f32[64]{0:T(128)S(1)}, f32[64]{0:T(128)S(1)}, f32[64,768]{1,0:T(8,128)S(1)}) fusion(f32[4,64,768]{2,1,0:T(8,128)S(1)} %get-tuple-element.552, s32[]{:T(128)S(6)} %select_n.44, f32[768]{0:T(1024)S(1)} %get-tuple-element.551, bf16[768,3072]{1,0:T(8,128)(2,1)} %get-tuple-element.550, f32[64,3072]{1,0:T(8,128)S(1)} %get-tuple-element.785, ...), kind=kOutput, calls=%fused_computation.553 | convolution fusion | flops 304938880 | bytes 6713856 | tf_op jit(solution)/shard_map/while/body/eval_jaxpr/cond/branch_1_fun/dot_general | solution.py:102
  232.4 1.1 bitcast_dynamic-update-slice_fusion
  233.4 1.3 collective-permute-start
  234.7 5.2 %collective-permute-done = bf16[64,768]{1,0:T(8,128)(2,1)S(1)} collective-permute-done((bf16[64,768]{1,0:T(8,128)(2,1)S(1)}, bf16[64,768]{1,0:T(8,128)(2,1)S(1)}, u32[]{:S(2)}, u32[]{:S(2)}) %collective-permute-start) | collective-permute-done | bytes 98336 | tf_op jit(solution)/shard_map/while/body/eval_jaxpr/ppermute | solution.py:17
  239.9 18.9 %conditional.2 = (bf16[64,768]{1,0:T(8,128)(2,1)S(1)}, bf16[4,64,768]{2,1,0:T(8,128)(2,1)S(1)}, f32[49,768]{1,0:T(8,128)S(1)}, f32[3072]{0:T(1024)S(1)}) conditional(s32[]{:T(128)} %convert_element_type.140, (bf16[4,64,768]{2,1,0:T(8,128)(2,1)S(1)}, f32[49,768]{1,0:T(8,128)S(1)}, f32[3072]{0:T(1024)S(1)}) %tuple.206, (pred[]{:T(512)}, s32[]{:T(128)}, ...), branch_computations={%region_3.3_spmd, %region_4.60_spmd} | conditional | flops 619948032 | bytes 28132316 | solution.py:180
  242.5 1.4 multiply_reduce_fusion.1
  245.1 4.1 %multiply_reduce_fusion = (f32[3072]{0:T(1024)S(1)}, f32[3072]{0:T(1024)S(1)}, f32[64,3072]{1,0:T(8,128)S(1)}) fusion(f32[3072]{0:T(1024)S(1)} %get-tuple-element.780, f32[4,64,3072]{2,1,0:T(8,128)} %get-tuple-element.548, s32[]{:T(128)S(6)} %select_n.44, bf16[3072,768]{1,0:T(8,128)(2,1)} %get-tuple-element.546, ...), kind=kOutput, calls=%fused_computation.61 | convolution fusion | flops 303605760 | bytes 6524937 | tf_op jit(solution)/shard_map/while/body/eval_jaxpr/cond/branch_1_fun/dot_general | solution.py:86
  250.6 4.4 %fusion.279 = (f32[64]{0:T(128)S(1)}, f32[64]{0:T(128)S(1)}, f32[64,768]{1,0:T(8,128)S(1)}) fusion(f32[4,64,768]{2,1,0:T(8,128)S(1)} %get-tuple-element.552, s32[]{:T(128)S(6)} %select_n.44, f32[768]{0:T(1024)S(1)} %get-tuple-element.551, bf16[768,3072]{1,0:T(8,128)(2,1)} %get-tuple-element.550, f32[64,3072]{1,0:T(8,128)S(1)} %get-tuple-element.785, ...), kind=kOutput, calls=%fused_computation.553 | convolution fusion | flops 304938880 | bytes 6713856 | tf_op jit(solution)/shard_map/while/body/eval_jaxpr/cond/branch_1_fun/dot_general | solution.py:102
  258.8 1.3 collective-permute-start
  260.1 5.2 %collective-permute-done = bf16[64,768]{1,0:T(8,128)(2,1)S(1)} collective-permute-done((bf16[64,768]{1,0:T(8,128)(2,1)S(1)}, bf16[64,768]{1,0:T(8,128)(2,1)S(1)}, u32[]{:S(2)}, u32[]{:S(2)}) %collective-permute-start) | collective-permute-done | bytes 98336 | tf_op jit(solution)/shard_map/while/body/eval_jaxpr/ppermute | solution.py:17
  265.5 20.8 %copy.11 = bf16[1,49,768]{0,1,2:T(8,128)(2,1)} copy(bf16[1,49,768]{2,0,1:T(2,128)(2,1)S(1)} %convert_element_type.114) | data formatting | bytes 150528
  286.2 10.2 %reshape_bitcast_fusion.1 = bf16[3072,1,1]{2,1,0:T(2,128)(2,1)S(1)} fusion(bf16[3072]{0:T(1024)(128)(2,1)S(1)} %convert_element_type.116), kind=kLoop, calls=%fused_computation.391 | loop fusion | bytes 12288
  297.6 9.4 %bitcast_reduce_fusion = bf16[768,49]{1,0:T(8,128)(2,1)} fusion(bf16[1,49,768]{0,1,2:T(8,128)(2,1)} %copy.11), kind=kLoop, calls=%fused_computation.387 | loop fusion | bytes 150528
  306.9 11.2 %reduce-scatter.9.cloned.1.call-done = bf16[768,1]{1,0:T(8,128)(2,1)} async-done(((bf16[3072,1]{1,0:T(8,128)(2,1)}), bf16[768,1]{1,0:T(8,128)(2,1)}) %reduce-scatter.9.cloned.1.call-update) | async-done | bytes 1552
  318.2 1.1 reduce.128
  319.3 2.6 reshape_bitcast_fusion.2
  322.8 17.6 %reduce-scatter.7.cloned.1.call-done = bf16[192,49]{1,0:T(8,128)(2,1)} async-done(((bf16[768,49]{1,0:T(8,128)(2,1)}), bf16[192,49]{1,0:T(8,128)(2,1)}) %reduce-scatter.7.cloned.1.call-update) | async-done | bytes 18832
  340.4 2.5 reshape_bitcast_fusion
  342.9 2.5 copy.12
  (323 shorter events, 24.9 us)
Async XLA Ops:
  7.2 9.8 %copy-start.3 = (bf16[1,3072]{1,0:T(2,128)(2,1)S(1)}, bf16[1,3072]{1,0:T(2,128)(2,1)}, u32[]{:S(2)}) copy-start(bf16[1,3072]{1,0:T(2,128)(2,1)} %param.17) | copy-start | bytes 18436
  7.2 9.9 %copy-start.4 = (bf16[1,768]{1,0:T(2,128)(2,1)S(1)}, bf16[1,768]{1,0:T(2,128)(2,1)}, u32[]{:S(2)}) copy-start(bf16[1,768]{1,0:T(2,128)(2,1)} %param.14) | copy-start | bytes 4612
  7.2 42.6 %all-gather.5.cloned.1.call-start = ((), (), s32[]{:S(2)}) async-start(), calls=%async_computation.3 | async-start | bytes 5898240 | tf_op jit(solution)/shard_map/all_gather | solution.py:130
  7.9 80.9 %all-gather.3.cloned.1.call-start = ((), (), s32[]{:S(2)}) async-start(), calls=%async_computation.2 | async-start | bytes 5898240 | tf_op jit(solution)/shard_map/all_gather | solution.py:131
  8.7 309.5 %reduce-scatter.9.cloned.1.call-start = ((), (), s32[]{:S(2)}) async-start(), calls=%async_computation.5 | async-start | bytes 983040
  17.2 71.7 %copy-start = (bf16[1,4,64,768]{3,2,1,0:T(8,128)(2,1)S(1)}, bf16[1,4,64,768]{3,2,1,0:T(8,128)(2,1)}, u32[]{:S(2)}) copy-start(bf16[1,4,64,768]{3,2,1,0:T(8,128)(2,1)} %param.12) | copy-start | bytes 1179652
  17.2 71.7 %copy-start.1 = (bf16[4,64,768]{2,1,0:T(8,128)(2,1)S(1)}, bf16[4,64,768]{2,1,0:T(8,128)(2,1)}, u32[]{:S(2)}) copy-start(bf16[4,64,768]{2,1,0:T(8,128)(2,1)} %param.18) | copy-start | bytes 1179652
  17.2 71.7 %copy-start.5 = (s32[1,4]{1,0:T(1,128)S(1)}, s32[1,4]{1,0:T(1,128)}, u32[]{:S(2)}) copy-start(s32[1,4]{1,0:T(1,128)} %param.19) | copy-start | bytes 52
  89.0 6.8 %collective-permute-start = (bf16[64,768]{1,0:T(8,128)(2,1)S(1)}, bf16[64,768]{1,0:T(8,128)(2,1)S(1)}, u32[]{:S(2)}, u32[]{:S(2)}) collective-permute-start(bf16[64,768]{1,0:T(8,128)(2,1)S(1)} %get-tuple-element.904), channel_id=1, source_target_pairs={{4,0},{8,4},{12,8},{5,1},{9,5},{13,9},{6,2},{10,6},{14,10},{7,3},{... | collective-permute-start | bytes 294920 | tf_op jit(solution)/shard_map/while/body/eval_jaxpr/ppermute | solution.py:17
  95.9 6.5 %collective-permute-start = (bf16[64,768]{1,0:T(8,128)(2,1)S(1)}, bf16[64,768]{1,0:T(8,128)(2,1)S(1)}, u32[]{:S(2)}, u32[]{:S(2)}) collective-permute-start(bf16[64,768]{1,0:T(8,128)(2,1)S(1)} %get-tuple-element.904), channel_id=1, source_target_pairs={{4,0},{8,4},{12,8},{5,1},{9,5},{13,9},{6,2},{10,6},{14,10},{7,3},{... | collective-permute-start | bytes 294920 | tf_op jit(solution)/shard_map/while/body/eval_jaxpr/ppermute | solution.py:17
  102.4 61.3 %collective-permute-start = (bf16[64,768]{1,0:T(8,128)(2,1)S(1)}, bf16[64,768]{1,0:T(8,128)(2,1)S(1)}, u32[]{:S(2)}, u32[]{:S(2)}) collective-permute-start(bf16[64,768]{1,0:T(8,128)(2,1)S(1)} %get-tuple-element.904), channel_id=1, source_target_pairs={{4,0},{8,4},{12,8},{5,1},{9,5},{13,9},{6,2},{10,6},{14,10},{7,3},{... | collective-permute-start | bytes 294920 | tf_op jit(solution)/shard_map/while/body/eval_jaxpr/ppermute | solution.py:17
  182.6 6.5 %collective-permute-start = (bf16[64,768]{1,0:T(8,128)(2,1)S(1)}, bf16[64,768]{1,0:T(8,128)(2,1)S(1)}, u32[]{:S(2)}, u32[]{:S(2)}) collective-permute-start(bf16[64,768]{1,0:T(8,128)(2,1)S(1)} %get-tuple-element.904), channel_id=1, source_target_pairs={{4,0},{8,4},{12,8},{5,1},{9,5},{13,9},{6,2},{10,6},{14,10},{7,3},{... | collective-permute-start | bytes 294920 | tf_op jit(solution)/shard_map/while/body/eval_jaxpr/ppermute | solution.py:17
  208.0 6.5 %collective-permute-start = (bf16[64,768]{1,0:T(8,128)(2,1)S(1)}, bf16[64,768]{1,0:T(8,128)(2,1)S(1)}, u32[]{:S(2)}, u32[]{:S(2)}) collective-permute-start(bf16[64,768]{1,0:T(8,128)(2,1)S(1)} %get-tuple-element.904), channel_id=1, source_target_pairs={{4,0},{8,4},{12,8},{5,1},{9,5},{13,9},{6,2},{10,6},{14,10},{7,3},{... | collective-permute-start | bytes 294920 | tf_op jit(solution)/shard_map/while/body/eval_jaxpr/ppermute | solution.py:17
  233.4 6.5 %collective-permute-start = (bf16[64,768]{1,0:T(8,128)(2,1)S(1)}, bf16[64,768]{1,0:T(8,128)(2,1)S(1)}, u32[]{:S(2)}, u32[]{:S(2)}) collective-permute-start(bf16[64,768]{1,0:T(8,128)(2,1)S(1)} %get-tuple-element.904), channel_id=1, source_target_pairs={{4,0},{8,4},{12,8},{5,1},{9,5},{13,9},{6,2},{10,6},{14,10},{7,3},{... | collective-permute-start | bytes 294920 | tf_op jit(solution)/shard_map/while/body/eval_jaxpr/ppermute | solution.py:17
  258.8 6.5 %collective-permute-start = (bf16[64,768]{1,0:T(8,128)(2,1)S(1)}, bf16[64,768]{1,0:T(8,128)(2,1)S(1)}, u32[]{:S(2)}, u32[]{:S(2)}) collective-permute-start(bf16[64,768]{1,0:T(8,128)(2,1)S(1)} %get-tuple-element.904), channel_id=1, source_target_pairs={{4,0},{8,4},{12,8},{5,1},{9,5},{13,9},{6,2},{10,6},{14,10},{7,3},{... | collective-permute-start | bytes 294920 | tf_op jit(solution)/shard_map/while/body/eval_jaxpr/ppermute | solution.py:17
  265.3 20.9 %copy-start.2 = (bf16[4,64,768]{2,1,0:T(8,128)(2,1)}, bf16[4,64,768]{2,1,0:T(8,128)(2,1)S(1)}, u32[]{:S(2)}) copy-start(bf16[4,64,768]{2,1,0:T(8,128)(2,1)S(1)} %get-tuple-element.587) | copy-start | bytes 1179652
  297.5 42.9 %reduce-scatter.7.cloned.1.call-start = ((), (), s32[]{:S(2)}) async-start(), calls=%async_computation.4 | async-start | bytes 245760
Sparse Core Ops, SparseCore 0:
  9.6 40.1 all-gather.4
  51.3 37.4 all-gather.2
  297.6 20.4 reduce-scatter.8
  320.6 19.7 reduce-scatter.6
where the time goes:
time: 354 us; the launch traced here: 353 us
  waiting for transfers between devices  188 us (53%)
  local copies, waits for them, and re-layouts  56.6 us (16%)
  matrix products  39.3 us (11%)
  other arithmetic  30.8 us (9%)
  loops' own time  14.8 us (4%)
  between operations  14 us (4%)
  starting transfers between devices  9.2 us (3%)
    ppermute x7, waiting for transfers between devices, from_behind(): lax.ppermute(value, axis, [(source, source + steps) for source in range(f...  91.6 us
    unnamed x20, local copies, waits for them, and re-layouts  49.4 us
    all_gather x1, waiting for transfers between devices, on_device(): lax.all_gather(shrink_weight, 'dp', axis=1, tiled=True)  33.6 us
    all_gather x1, waiting for transfers between devices, on_device(): lax.all_gather(expand_weight, 'dp', axis=1, tiled=True)  32.5 us
    unnamed x6, waiting for transfers between devices  30.3 us
    dot_general x4, matrix products, block_backward(): lax.dot_general(back_hidden, expand, (((1,), (1,)), ((), ())), preferred_...  17.4 us
    dot_general x4, matrix products, block_backward(): lax.dot_general(upstream, shrink, (((1,), (1,)), ((), ())), preferred_ele...  16.5 us
    another operation x7, loops' own time, advance(): lax.cond(active, run_section, pass_over, (upstream, member, result, kern_...  14.6 us
  transfers between devices with their start and end apart: 11, of which 11 were waited for; matrix products, arithmetic and copies ran while one was open for 8% of the time, Pallas kernels for 0%

commit v1 on v0

v1 whole, which is shorter than its diff:
```python
import functools

import jax
import jax.numpy as jnp
from jax import lax
from jax.experimental import pallas as pl
from jax.experimental.pallas import tpu as pltpu
from jax.sharding import PartitionSpec as P

KSIDE = 7
SIDE = 8
MARGIN = 3
TAPS = KSIDE * KSIDE
LANES = 128
WINDOW = 256

inverse_root_two = 0.7071067811865476
inverse_root_tau = 0.3989422804014327

MESH = pl.DeviceIdType.MESH
CHUNKS = 3
F_BLOCK = 512
NT = (((1,), (1,)), ((), ()))


def shifted(value, by):
    if by == 0:
        return value
    column = lax.broadcasted_iota(jnp.int32, value.shape, 1) + by
    moved = pltpu.roll(value, (-by) % SIDE, 1)
    return jnp.where((column >= 0) & (column < SIDE), moved, 0.0)


def row_padded(value):
    zeros = jnp.zeros((MARGIN,) + value.shape[1:], value.dtype)
    return jnp.concatenate([zeros, value, zeros], axis=0)


def kernel(
    sections,
    x_ref,
    tap_ref,
    gain_ref,
    expand_ref,
    shrink_ref,
    resp_ref,
    loss_ref,
    grad_ref,
    share_ref,
    ew,
    sw,
    taps,
    mixed,
    normed,
    spread,
    scaled,
    hid,
    act,
    energy,
    ratio,
    sums,
    back,
    back_hid,
    side_steps,
    tap_acc,
    resp_acc,
    inbox,
    stage,
    landed,
    local_sem,
    x_send,
    x_recv,
    y_send,
    y_recv,
    own_send,
    own_recv,
    f_send,
    f_recv,
    h_send,
    h_recv,
    p_send,
    p_recv,
    s_send,
    s_recv,
):
    micro, pix, channels = x_ref.shape
    units = sw.shape[0]
    e_rows, s_rows = expand_ref.shape[0], shrink_ref.shape[0]
    grp = lax.axis_index("groups")
    pos = lax.axis_index("pipe")
    me = lax.axis_index("dp")
    last = sections - 1
    high, low = me // 2, me % 2
    across = 2 * (1 - high) + low
    beside = 2 * high + (1 - low)
    other = 2 * (1 - high) + (1 - low)

    barrier = pltpu.get_barrier_semaphore()

    def greet(g, p, d):
        pl.semaphore_signal(barrier, inc=1, device_id=(g, p, d), device_id_type=MESH)

    greet(grp, pos, across)
    greet(grp, pos, beside)
    greet(grp, pos, other)
    greet(1 - grp, pos, me)

    @pl.when(pos > 0)
    def _():
        greet(grp, pos - 1, me)

    @pl.when(pos < last)
    def _():
        greet(grp, pos + 1, me)

    pl.semaphore_wait(
        barrier, 4 + jnp.where(pos > 0, 1, 0) + jnp.where(pos < last, 1, 0)
    )

    def piece(owner, half, c):
        if c < CHUNKS:
            size = e_rows // (2 * CHUNKS)
            start = owner * e_rows + half * (e_rows // 2) + c * size
            return ew.at[pl.ds(pl.multiple_of(start, 16), size), :]
        size = s_rows // (2 * CHUNKS)
        start = owner * s_rows + half * (s_rows // 2) + (c - CHUNKS) * size
        return sw.at[pl.ds(pl.multiple_of(start, 16), size), :]

    def own_piece(half, c):
        if c < CHUNKS:
            size = e_rows // (2 * CHUNKS)
            start = half * (e_rows // 2) + c * size
            return expand_ref.at[pl.ds(pl.multiple_of(start, 16), size), :]
        size = s_rows // (2 * CHUNKS)
        start = half * (s_rows // 2) + (c - CHUNKS) * size
        return shrink_ref.at[pl.ds(pl.multiple_of(start, 16), size), :]

    def remote(src, dst, send, recv, g, p, d):
        return pltpu.make_async_remote_copy(
            src_ref=src,
            dst_ref=dst,
            send_sem=send,
            recv_sem=recv,
            device_id=(g, p, d),
            device_id_type=MESH,
        )

    def x_copy(c, owner):
        return remote(
            own_piece(grp, c), piece(owner, grp, c), x_send.at[c], x_recv.at[c], grp, pos, across
        )

    def y_copy(c, half):
        spot = piece(across, half, c)
        return remote(spot, spot, y_send.at[c], y_recv.at[c], 1 - grp, pos, me)

    def f_copy(c, owner):
        spot = piece(owner, grp, c)
        return remote(spot, spot, f_send.at[c], f_recv.at[c], grp, pos, beside)

    def h_copy(c, owner):
        spot = piece(owner, 1 - grp, c)
        return remote(spot, spot, h_send.at[c], h_recv.at[c], grp, pos, beside)

    def shard(which, owner):
        if which == 0:
            return ew.at[pl.ds(pl.multiple_of(owner * e_rows, 16), e_rows), :]
        return sw.at[pl.ds(pl.multiple_of(owner * s_rows, 16), s_rows), :]

    def own_copy(which, owner):
        src = (expand_ref, shrink_ref)[which]
        return remote(
            src, shard(which, owner), own_send.at[which], own_recv.at[which], grp, pos, beside
        )

    for c in range(2 * CHUNKS):
        x_copy(c, me).start()
    for which in range(2):
        own_copy(which, me).start()
    locals_ = [
        pltpu.make_async_copy((expand_ref, shrink_ref)[w], shard(w, me), local_sem.at[w])
        for w in range(2)
    ]
    for copy in locals_:
        copy.start()

    def pass_x(c):
        x_copy(c, across).wait_recv()
        y_copy(c, grp).start()
        f_copy(c, across).start()

    def pass_y(c):
        y_copy(c, 1 - grp).wait_recv()
        h_copy(c, across).start()

    taps[...] = tap_ref[...].astype(jnp.float32)
    gain = gain_ref[...].astype(jnp.float32)

    def forward(slot):
        def tile(t, carry):
            lanes = pl.ds(pl.multiple_of(t * LANES, LANES), LANES)
            image = x_ref[slot, :, lanes].astype(jnp.float32).reshape(SIDE, SIDE, LANES)
            total = jnp.zeros_like(image)
            for col in range(KSIDE):
                moved = row_padded(shifted(image, col - MARGIN))
                for row in range(KSIDE):
                    tap = row * KSIDE + col
                    total = total + taps[tap : tap + 1, lanes][None] * moved[row : row + SIDE]
            mixed[:, lanes] = total.reshape(pix, LANES)
            return carry

        lax.fori_loop(0, channels // LANES, tile, 0)
        value = mixed[...]
        offset = value - jnp.mean(value, axis=-1, keepdims=True)
        scale = lax.rsqrt(jnp.mean(offset * offset, axis=-1, keepdims=True) + 1e-06)
        unit = offset * scale
        normed[slot] = unit
        spread[slot] = scale
        scaled[pl.ds(pl.multiple_of(slot * pix, pix), pix), :] = (unit * gain).astype(jnp.bfloat16)

    def forward_step(slot, carry):
        forward(slot)
        return carry

    lax.fori_loop(0, micro, forward_step, 0)
    tap_acc[...] = jnp.zeros_like(tap_acc)
    resp_acc[...] = jnp.zeros_like(resp_acc)

    pass_x(0)
    for c in range(1, CHUNKS + 1):
        pass_x(c)
        pass_y(c - 1)
    locals_[0].wait()
    own_copy(0, beside).wait_recv()
    for c in range(CHUNKS):
        f_copy(c, other).wait_recv()
        h_copy(c, other).wait_recv()

    def hidden_block(b, carry):
        cols = pl.ds(pl.multiple_of(b * F_BLOCK, F_BLOCK), F_BLOCK)
        result = jnp.dot(scaled[...], ew[:, cols], preferred_element_type=jnp.float32)
        hid[:, :, cols] = result.reshape(micro, pix, F_BLOCK)
        return carry

    lax.fori_loop(0, units // F_BLOCK, hidden_block, 0)

    resp_block = F_BLOCK

    def gelu(slot):
        def block(b, carry):
            cols = pl.ds(pl.multiple_of(b * resp_block, resp_block), resp_block)
            h = hid[slot, :, cols]
            erf_part = 0.5 * (1.0 + lax.erf(h * inverse_root_two))
            a = h * erf_part
            act[slot, :, cols] = a
            hid[slot, :, cols] = erf_part + h * jnp.exp(-0.5 * h * h) * inverse_root_tau
            energy[slot, :, cols] = jnp.sqrt(jnp.sum(a * a, axis=0, keepdims=True) + 1e-06)
            return carry

        lax.fori_loop(0, units // resp_block, block, 0)
        e = energy[slot]
        ratio[slot] = e / (jnp.mean(e, axis=-1, keepdims=True) + 1e-06)

    pending = [c for c in range(CHUNKS + 1, 2 * CHUNKS)]
    for slot in range(micro):
        gelu(slot)
        if pending:
            c = pending.pop(0)
            pass_x(c)
            pass_y(c - 1)
    for c in pending:
        pass_x(c)
        pass_y(c - 1)
    pass_y(2 * CHUNKS - 1)
    locals_[1].wait()
    own_copy(1, beside).wait_recv()
    for c in range(CHUNKS, 2 * CHUNKS):
        f_copy(c, other).wait_recv()
        h_copy(c, other).wait_recv()

    def give(slot):
        return remote(
            grad_ref.at[slot], inbox.at[slot], p_send.at[slot], p_recv.at[slot], grp, pos - 1, me
        )

    def take(slot):
        return remote(
            grad_ref.at[slot], inbox.at[slot], p_send.at[slot], p_recv.at[slot], grp, pos + 1, me
        )

    def backward(slot, carry):
        @pl.when(pos == last)
        def _():
            inbox[slot] = loss_ref[slot]

        @pl.when(pos < last)
        def _():
            take(slot).wait_recv()

        up = inbox[slot]
        average = jnp.mean(energy[slot], axis=-1, keepdims=True) + 1e-06
        weight = jnp.zeros((1, 1), jnp.float32)
        for b in range(units // F_BLOCK):
            cols = slice(b * F_BLOCK, (b + 1) * F_BLOCK)
            br = lax.dot_general(up, sw[cols, :], NT, preferred_element_type=jnp.float32)
            back[:, cols] = br
            s = jnp.sum(br * act[slot, :, cols], axis=0, keepdims=True)
            resp_acc[:, cols] += s * ratio[slot, :, cols]
            w = s * resp_ref[:, cols].astype(jnp.float32)
            sums[:, cols] = w
            weight += jnp.sum(w * energy[slot, :, cols], axis=-1, keepdims=True)
        weight = weight / (average * average * units)
        inverse = 1.0 / average
        for b in range(units // F_BLOCK):
            cols = slice(b * F_BLOCK, (b + 1) * F_BLOCK)
            first = 1.0 + resp_ref[:, cols].astype(jnp.float32) * ratio[slot, :, cols]
            second = (sums[:, cols] * inverse - weight) / energy[slot, :, cols]
            ba = back[:, cols] * first + act[slot, :, cols] * second
            back_hid[:, cols] = (ba * hid[slot, :, cols]).astype(jnp.bfloat16)
        bs = jnp.zeros((pix, channels), jnp.float32)
        for b in range(units // F_BLOCK):
            cols = slice(b * F_BLOCK, (b + 1) * F_BLOCK)
            bs += lax.dot_general(
                back_hid[:, cols], ew[:, cols], NT, preferred_element_type=jnp.float32
            )
        q = bs * gain
        unit = normed[slot]
        mixed[...] = (
            q
            - jnp.mean(q, axis=-1, keepdims=True)
            - unit * jnp.mean(q * unit, axis=-1, keepdims=True)
        ) * spread[slot]

        def tile(t, inner):
            lanes = pl.ds(pl.multiple_of(t * LANES, LANES), LANES)
            image = mixed[:, lanes].reshape(SIDE, SIDE, LANES)
            total = inbox[slot, :, lanes].astype(jnp.float32).reshape(SIDE, SIDE, LANES)
            for col in range(KSIDE):
                plain = shifted(image, MARGIN - col)
                side_steps[col, :, lanes] = plain.reshape(pix, LANES)
                moved = row_padded(plain)
                for row in range(KSIDE):
                    tap = row * KSIDE + col
                    at = KSIDE - 1 - row
                    total = total + taps[tap : tap + 1, lanes][None] * moved[at : at + SIDE]
            grad_ref[slot, :, lanes] = total.reshape(pix, LANES).astype(jnp.bfloat16)
            return inner

        lax.fori_loop(0, channels // LANES, tile, 0)

        @pl.when(pos > 0)
        def _():
            give(slot).start()

        def tap_tile(t, inner):
            lanes = pl.ds(pl.multiple_of(t * LANES, LANES), LANES)
            image = x_ref[slot, :, lanes].astype(jnp.float32).reshape(SIDE, SIDE, LANES)
            for col in range(KSIDE):
                moved = row_padded(side_steps[col, :, lanes].reshape(SIDE, SIDE, LANES))
                for row in range(KSIDE):
                    tap = row * KSIDE + col
                    at = KSIDE - 1 - row
                    tap_acc[tap, :, lanes] += jnp.sum(moved[at : at + SIDE] * image, axis=0)
            return inner

        lax.fori_loop(0, channels // LANES, tap_tile, 0)
        return carry

    lax.fori_loop(0, micro, backward, 0)

    totals = jnp.sum(tap_acc[...], axis=1)
    share = channels // 4
    pad = stage.shape[1] - TAPS - units // 4 // WINDOW
    for d in range(4):
        start = d * share // LANES * LANES
        rows = [totals[:, start : start + WINDOW]]
        for k in range(units // 4 // WINDOW):
            at = d * (units // 4) + k * WINDOW
            rows.append(resp_acc[:, at : at + WINDOW])
        rows.append(jnp.zeros((pad, WINDOW), jnp.float32))
        stage[d] = jnp.concatenate(rows, axis=0).astype(jnp.bfloat16)

    peers = (across, beside, other)

    def s_copy(k):
        return remote(stage.at[peers[k]], landed.at[k], s_send.at[k], s_recv.at[k], grp, pos, peers[k])

    for k in range(3):
        s_copy(k).start()
    total = stage[me].astype(jnp.float32)
    for k in range(3):
        s_copy(k).wait_recv()
        total = total + landed[k].astype(jnp.float32)
    share_ref[...] = total

    for k in range(3):
        s_copy(k).wait_send()
    for c in range(2 * CHUNKS):
        x_copy(c, me).wait_send()
        y_copy(c, grp).wait_send()
        f_copy(c, across).wait_send()
        h_copy(c, across).wait_send()
    for which in range(2):
        own_copy(which, me).wait_send()

    @pl.when(pos > 0)
    def _():
        def drain(slot, carry):
            give(slot).wait_send()
            return carry

        lax.fori_loop(0, micro, drain, 0)


def on_device(
    section_input,
    depth_kernel,
    norm_gain,
    expand_weight,
    shrink_weight,
    response_gain,
    loss_grad,
    plan,
):
    local_x = section_input[0]
    micro, pix, channels = local_x.shape
    units = expand_weight.shape[2]
    sections = lax.axis_size("pipe")
    me = lax.axis_index("dp")
    order = plan[0]

    def pick(value, index):
        return lax.dynamic_index_in_dim(value, index, 0, keepdims=False)

    arranged = jnp.stack([pick(local_x, order[j]) for j in range(micro)])
    f32, bf16 = jnp.float32, jnp.bfloat16
    vmem = pl.BlockSpec(memory_space=pltpu.VMEM)
    anywhere = pl.BlockSpec(memory_space=pl.ANY)
    dma = pltpu.SemaphoreType.DMA
    grads, shares = pl.pallas_call(
        functools.partial(kernel, sections),
        out_shape=(
            jax.ShapeDtypeStruct((micro, pix, channels), bf16),
            jax.ShapeDtypeStruct((64, WINDOW), f32),
        ),
        in_specs=[vmem, vmem, vmem, anywhere, anywhere, vmem, vmem],
        out_specs=(vmem, vmem),
        scratch_shapes=[
            pltpu.VMEM((channels, units), bf16),
            pltpu.VMEM((units, channels), bf16),
            pltpu.VMEM((TAPS, channels), f32),
            pltpu.VMEM((pix, channels), f32),
            pltpu.VMEM((micro, pix, channels), f32),
            pltpu.VMEM((micro, pix, 1), f32),
            pltpu.VMEM((micro * pix, channels), bf16),
            pltpu.VMEM((micro, pix, units), f32),
            pltpu.VMEM((micro, pix, units), f32),
            pltpu.VMEM((micro, 1, units), f32),
            pltpu.VMEM((micro, 1, units), f32),
            pltpu.VMEM((1, units), f32),
            pltpu.VMEM((pix, units), f32),
            pltpu.VMEM((pix, units), bf16),
            pltpu.VMEM((KSIDE, pix, channels), f32),
            pltpu.VMEM((TAPS, SIDE, channels), f32),
            pltpu.VMEM((1, units), f32),
            pltpu.VMEM((micro, pix, channels), bf16),
            pltpu.VMEM((4, 64, WINDOW), bf16),
            pltpu.VMEM((3, 64, WINDOW), bf16),
            dma((2,)),
            dma((2 * CHUNKS,)),
            dma((2 * CHUNKS,)),
            dma((2 * CHUNKS,)),
            dma((2 * CHUNKS,)),
            dma((2,)),
            dma((2,)),
            dma((2 * CHUNKS,)),
            dma((2 * CHUNKS,)),
            dma((2 * CHUNKS,)),
            dma((2 * CHUNKS,)),
            dma((micro,)),
            dma((micro,)),
            dma((3,)),
            dma((3,)),
        ],
        compiler_params=pltpu.CompilerParams(
            collective_id=0, has_side_effects=True, vmem_limit_bytes=52 * 1024 * 1024
        ),
    )(
        arranged,
        depth_kernel[0],
        norm_gain,
        expand_weight[0],
        shrink_weight[0],
        response_gain,
        loss_grad,
    )
    slots = jnp.arange(micro, dtype=jnp.int32)
    result = jnp.stack(
        [pick(grads, jnp.sum(jnp.where(order == m, slots, 0))) for m in range(micro)]
    )
    share = channels // 4
    start = me * share - me * share // LANES * LANES
    kern_share = lax.dynamic_slice(shares, (0, start), (TAPS, share))
    gain_share = shares[TAPS : TAPS + units // 4 // WINDOW].reshape(1, units // 4)
    return (result[None], kern_share[None], gain_share)


def solution(mesh):
    if mesh.shape["dp"] != 4 or mesh.shape["groups"] != 2:
        raise ValueError("unsupported mesh")
    placed = (
        P("pipe", ("groups", "dp"), None, None),
        P("pipe", None, None),
        P("pipe", None),
        P("pipe", "dp", None),
        P("pipe", "dp", None),
        P("pipe", None),
        P(("groups", "dp"), None, None),
        P(("groups", "dp"), None),
    )
    return jax.shard_map(
        on_device,
        mesh=mesh,
        in_specs=placed,
        out_specs=(
            P("pipe", ("groups", "dp"), None, None),
            P(("groups", "pipe"), None, "dp"),
            P(("groups", "pipe"), "dp"),
        ),
        check_vma=False,
    )
```

time: 354 us -> 114 us (0.32)
  waiting for transfers between devices: 188 us -> 0 us
  Pallas kernels: 0 us -> 92 us
  local copies, waits for them, and re-layouts: 56.6 us -> 3.93 us
  matrix products: 39.3 us -> 0 us
  other arithmetic: 30.8 us -> 1.6 us
  loops' own time: 14.8 us -> 0 us
  starting transfers between devices: 9.2 us -> 0 us
    pallas_call x0 -> x1, Pallas kernels: none -> 92 us  [on_device(): pl.pallas_call(functools.partial(kernel, sections), out_shape=(jax.ShapeD...]
    ppermute x7 -> x0, waiting for transfers between devices: 91.6 us -> none  [from_behind(): lax.ppermute(value, axis, [(source, source + steps) for source in range(f...]
    all_gather x2 -> x0, waiting for transfers between devices: 66.2 us -> none  [the longest x1 33.6 us: on_device(): lax.all_gather(shrink_weight, 'dp', axis=1, tiled=True)]
    unnamed x20 -> x12, local copies, waits for them, and re-layouts: 49.4 us -> 0.61 us
    dot_general x9 -> x0, matrix products: 39.3 us -> none  [the longest x4 17.4 us: block_backward(): lax.dot_general(back_hidden, expand, (((1,), (1,)), ((), ())), preferred_...]
    unnamed x6 -> x0, waiting for transfers between devices: 30.3 us -> none
    reduce_sum x30 -> x1, other arithmetic: 21.5 us -> 0.75 us  [on_device(): jnp.sum(jnp.where(order == m, slots, 0))]
    another operation x8 -> x0, loops' own time: 14.8 us -> none  [the longest x7 14.6 us: advance(): lax.cond(active, run_section, pass_over, (upstream, member, result, kern_...]
  transfers between devices with their start and end apart: 11 -> 0, of which waited for: 11 -> 0; matrix products, arithmetic and copies ran while one was open for 8% -> 0% of each run, Pallas kernels for 0% -> 0%
where the time goes in v1:
time: 114 us
  Pallas kernels  92 us (81%)
  between operations  16.5 us (14%)
  local copies, waits for them, and re-layouts  3.93 us (3%)
  other arithmetic  1.6 us (1%)
    pallas_call x1, Pallas kernels, on_device(): pl.pallas_call(functools.partial(kernel, sections), out_shape=(jax.ShapeD...  92 us

profile of v1, /device:TPU:0, one launch (start us, length us, event | category | flops | bytes accessed | tf_op | source)
XLA Modules:
  0.0 114.1 jit_solution(8244200135135912378)
XLA Ops:
  0.6 0.0 copy-start.1
  0.6 0.0 copy-start.3
  0.7 0.0 copy-start.2
  0.7 0.0 copy-start
  0.7 1.5 %fusion.4 = (s32[1,1]{1,0:T(1,128)}, s32[1,1]{1,0:T(1,128)}, s32[1,1]{1,0:T(1,128)}, s32[1,1]{1,0:T(1,128)}) fusion(s32[1,4]{1,0:T(1,128)} %param.15), kind=kLoop, calls=%fused_computation.20 | loop fusion | bytes 32 | tf_op jit(solution)/shard_map/slice | solution.py:435
  10.0 1.1 dynamic-slice_bitcast_fusion.3
  11.1 0.1 pad_maximum_fusion.x_ref
  11.2 0.0 copy-done.1
  11.2 0.0 copy-done.3
  11.2 0.0 copy-done.2
  11.2 0.0 copy-done
  11.2 0.0 copy-start.4
  11.2 92.0 %shard_map.103 = (bf16[4,64,768]{2,1,0:T(8,128)(2,1)S(1)}, f32[64,256]{1,0:T(8,128)S(1)}) custom-call(bf16[4,64,768]{2,1,0:T(8,128)(2,1)S(1)} %pad_maximum_fusion.x_ref, bf16[49,768]{1,0:T(8,128)(2,1)S(1)} %bitcast.37, bf16[1,768]{1,0:T(2,128)(2,1)S(1)} %copy-done.3, bf16[192,3072]{1,0:T(8,128)(2,1)} %bitcast.38, bf16[768,768]{1,0:T(8,128)(2,1)} %bitcast.39, ...), custom_call_target="tpu_custom_call" | custom-call | tf_op jit(solution)/shard_map/pallas_call | solution.py:440
  103.2 0.0 copy-done.4
  103.3 0.8 fusion
  111.9 0.8 maximum_bitcast_fusion
  112.7 0.1 constant_dynamic-slice_fusion
  112.8 0.7 broadcast_in_dim.12
  113.5 0.6 copy.11
  (2 shorter events, 0.0 us)
Async XLA Ops:
  0.6 10.5 %copy-start.1 = (bf16[1,49,768]{2,1,0:T(8,128)(2,1)S(1)}, bf16[1,49,768]{2,1,0:T(8,128)(2,1)}, u32[]{:S(2)}) copy-start(bf16[1,49,768]{2,1,0:T(8,128)(2,1)} %param.9) | copy-start | bytes 225796
  0.6 10.5 %copy-start.3 = (bf16[1,768]{1,0:T(2,128)(2,1)S(1)}, bf16[1,768]{1,0:T(2,128)(2,1)}, u32[]{:S(2)}) copy-start(bf16[1,768]{1,0:T(2,128)(2,1)} %gain_ref.1) | copy-start | bytes 4612
  0.7 10.5 %copy-start.2 = (bf16[1,3072]{1,0:T(2,128)(2,1)S(1)}, bf16[1,3072]{1,0:T(2,128)(2,1)}, u32[]{:S(2)}) copy-start(bf16[1,3072]{1,0:T(2,128)(2,1)} %resp_ref.1) | copy-start | bytes 18436
  0.7 10.5 %copy-start = (bf16[4,64,768]{2,1,0:T(8,128)(2,1)S(1)}, bf16[4,64,768]{2,1,0:T(8,128)(2,1)}, u32[]{:S(2)}) copy-start(bf16[4,64,768]{2,1,0:T(8,128)(2,1)} %loss_ref.1) | copy-start | bytes 1179652
  11.2 92.0 %copy-start.4 = (s32[1,4]{1,0:T(1,128)S(1)}, s32[1,4]{1,0:T(1,128)}, u32[]{:S(2)}) copy-start(s32[1,4]{1,0:T(1,128)} %param.15) | copy-start | bytes 52

commit v2 on v1

--- a/solution.py
+++ b/solution.py
@@ -13,12 +13,13 @@
 TAPS = KSIDE * KSIDE
 LANES = 128
 WINDOW = 256
+PIECES = 3
 
 inverse_root_two = 0.7071067811865476
 inverse_root_tau = 0.3989422804014327
 
 MESH = pl.DeviceIdType.MESH
-CHUNKS = 3
+CHUNKS = 6
 F_BLOCK = 512
 NT = (((1,), (1,)), ((), ()))
 
@@ -38,6 +39,7 @@
 
 def kernel(
     sections,
+    plan_ref,
     x_ref,
     tap_ref,
     gain_ref,
@@ -45,8 +47,10 @@
     shrink_ref,
     resp_ref,
     loss_ref,
+    out_ref,
+    tap_out,
+    resp_out,
     grad_ref,
-    share_ref,
     ew,
     sw,
     taps,
@@ -199,7 +203,7 @@
     def forward(slot):
         def tile(t, carry):
             lanes = pl.ds(pl.multiple_of(t * LANES, LANES), LANES)
-            image = x_ref[slot, :, lanes].astype(jnp.float32).reshape(SIDE, SIDE, LANES)
+            image = x_ref[plan_ref[0, slot], :, lanes].astype(jnp.float32).reshape(SIDE, SIDE, LANES)
             total = jnp.zeros_like(image)
             for col in range(KSIDE):
                 moved = row_padded(shifted(image, col - MARGIN))
@@ -218,18 +222,21 @@
         spread[slot] = scale
         scaled[pl.ds(pl.multiple_of(slot * pix, pix), pix), :] = (unit * gain).astype(jnp.bfloat16)
 
-    def forward_step(slot, carry):
-        forward(slot)
-        return carry
-
-    lax.fori_loop(0, micro, forward_step, 0)
     tap_acc[...] = jnp.zeros_like(tap_acc)
     resp_acc[...] = jnp.zeros_like(resp_acc)
 
-    pass_x(0)
-    for c in range(1, CHUNKS + 1):
-        pass_x(c)
-        pass_y(c - 1)
+    def passes(steps, count):
+        for c in steps[:count]:
+            pass_x(c)
+            if c > 0:
+                pass_y(c - 1)
+        return steps[count:]
+
+    first_part = list(range(CHUNKS + 1))
+    for slot in range(micro):
+        forward(slot)
+        first_part = passes(first_part, 1)
+    passes(first_part, CHUNKS)
     locals_[0].wait()
     own_copy(0, beside).wait_recv()
     for c in range(CHUNKS):
@@ -243,6 +250,7 @@
         return carry
 
     lax.fori_loop(0, units // F_BLOCK, hidden_block, 0)
+    second_part = passes(list(range(CHUNKS + 1, 2 * CHUNKS)), 1)
 
     resp_block = F_BLOCK
 
@@ -261,16 +269,10 @@
         e = energy[slot]
         ratio[slot] = e / (jnp.mean(e, axis=-1, keepdims=True) + 1e-06)
 
-    pending = [c for c in range(CHUNKS + 1, 2 * CHUNKS)]
     for slot in range(micro):
         gelu(slot)
-        if pending:
-            c = pending.pop(0)
-            pass_x(c)
-            pass_y(c - 1)
-    for c in pending:
-        pass_x(c)
-        pass_y(c - 1)
+        second_part = passes(second_part, 1)
+    passes(second_part, CHUNKS)
     pass_y(2 * CHUNKS - 1)
     locals_[1].wait()
     own_copy(1, beside).wait_recv()
@@ -278,14 +280,12 @@
         f_copy(c, other).wait_recv()
         h_copy(c, other).wait_recv()
 
-    def give(slot):
+    width = channels // PIECES
+
+    def pipe_copy(slot, k, to):
+        spot = (slot, slice(None), slice(k * width, (k + 1) * width))
         return remote(
-            grad_ref.at[slot], inbox.at[slot], p_send.at[slot], p_recv.at[slot], grp, pos - 1, me
-        )
-
-    def take(slot):
-        return remote(
-            grad_ref.at[slot], inbox.at[slot], p_send.at[slot], p_recv.at[slot], grp, pos + 1, me
+            grad_ref.at[spot], inbox.at[spot], p_send.at[slot, k], p_recv.at[slot, k], grp, to, me
         )
 
     def backward(slot, carry):
@@ -295,7 +295,8 @@
 
         @pl.when(pos < last)
         def _():
-            take(slot).wait_recv()
+            for k in range(PIECES):
+                pipe_copy(slot, k, pos + 1).wait_recv()
 
         up = inbox[slot]
         average = jnp.mean(energy[slot], axis=-1, keepdims=True) + 1e-06
@@ -346,15 +347,16 @@
             grad_ref[slot, :, lanes] = total.reshape(pix, LANES).astype(jnp.bfloat16)
             return inner
 
-        lax.fori_loop(0, channels // LANES, tile, 0)
-
-        @pl.when(pos > 0)
-        def _():
-            give(slot).start()
+        for k in range(PIECES):
+            lax.fori_loop(k * width // LANES, (k + 1) * width // LANES, tile, 0)
+
+            @pl.when(pos > 0)
+            def _():
+                pipe_copy(slot, k, pos - 1).start()
 
         def tap_tile(t, inner):
             lanes = pl.ds(pl.multiple_of(t * LANES, LANES), LANES)
-            image = x_ref[slot, :, lanes].astype(jnp.float32).reshape(SIDE, SIDE, LANES)
+            image = x_ref[plan_ref[0, slot], :, lanes].astype(jnp.float32).reshape(SIDE, SIDE, LANES)
             for col in range(KSIDE):
                 moved = row_padded(side_steps[col, :, lanes].reshape(SIDE, SIDE, LANES))
                 for row in range(KSIDE):
@@ -387,11 +389,20 @@
 
     for k in range(3):
         s_copy(k).start()
+    for m in range(micro):
+        slot = jnp.int32(0)
+        for j in range(1, micro):
+            slot = jnp.where(plan_ref[0, j] == m, j, slot)
+        out_ref[m] = grad_ref[slot]
     total = stage[me].astype(jnp.float32)
     for k in range(3):
         s_copy(k).wait_recv()
         total = total + landed[k].astype(jnp.float32)
-    share_ref[...] = total
+    edge = share - share // LANES * LANES
+    odd = me * share % LANES != 0
+    tap_out[...] = jnp.where(odd, total[:TAPS, edge : edge + share], total[:TAPS, :share])
+    for k in range(units // 4 // WINDOW):
+        resp_out[:, k * WINDOW : (k + 1) * WINDOW] = total[TAPS + k : TAPS + k + 1]
 
     for k in range(3):
         s_copy(k).wait_send()
@@ -406,7 +417,8 @@
     @pl.when(pos > 0)
     def _():
         def drain(slot, carry):
-            give(slot).wait_send()
+            for k in range(PIECES):
+                pipe_copy(slot, k, pos - 1).wait_send()
             return carry
 
         lax.fori_loop(0, micro, drain, 0)
@@ -426,26 +438,23 @@
     micro, pix, channels = local_x.shape
     units = expand_weight.shape[2]
     sections = lax.axis_size("pipe")
-    me = lax.axis_index("dp")
-    order = plan[0]
-
-    def pick(value, index):
-        return lax.dynamic_index_in_dim(value, index, 0, keepdims=False)
-
-    arranged = jnp.stack([pick(local_x, order[j]) for j in range(micro)])
+    share = channels // 4
     f32, bf16 = jnp.float32, jnp.bfloat16
     vmem = pl.BlockSpec(memory_space=pltpu.VMEM)
+    smem = pl.BlockSpec(memory_space=pltpu.SMEM)
     anywhere = pl.BlockSpec(memory_space=pl.ANY)
     dma = pltpu.SemaphoreType.DMA
-    grads, shares = pl.pallas_call(
+    grads, tap_share, resp_share = pl.pallas_call(
         functools.partial(kernel, sections),
         out_shape=(
             jax.ShapeDtypeStruct((micro, pix, channels), bf16),
-            jax.ShapeDtypeStruct((64, WINDOW), f32),
+            jax.ShapeDtypeStruct((TAPS, share), f32),
+            jax.ShapeDtypeStruct((1, units // 4), f32),
         ),
-        in_specs=[vmem, vmem, vmem, anywhere, anywhere, vmem, vmem],
-        out_specs=(vmem, vmem),
+        in_specs=[smem, vmem, vmem, vmem, anywhere, anywhere, vmem, vmem],
+        out_specs=(vmem, vmem, vmem),
         scratch_shapes=[
+            pltpu.VMEM((micro, pix, channels), bf16),
             pltpu.VMEM((channels, units), bf16),
             pltpu.VMEM((units, channels), bf16),
             pltpu.VMEM((TAPS, channels), f32),
@@ -477,8 +486,8 @@
             dma((2 * CHUNKS,)),
             dma((2 * CHUNKS,)),
             dma((2 * CHUNKS,)),
-            dma((micro,)),
-            dma((micro,)),
+            dma((micro, PIECES)),
+            dma((micro, PIECES)),
             dma((3,)),
             dma((3,)),
         ],
@@ -486,7 +495,8 @@
             collective_id=0, has_side_effects=True, vmem_limit_bytes=52 * 1024 * 1024
         ),
     )(
-        arranged,
+        plan,
+        local_x,
         depth_kernel[0],
         norm_gain,
         expand_weight[0],
@@ -494,15 +504,7 @@
         response_gain,
         loss_grad,
     )
-    slots = jnp.arange(micro, dtype=jnp.int32)
-    result = jnp.stack(
-        [pick(grads, jnp.sum(jnp.where(order == m, slots, 0))) for m in range(micro)]
-    )
-    share = channels // 4
-    start = me * share - me * share // LANES * LANES
-    kern_share = lax.dynamic_slice(shares, (0, start), (TAPS, share))
-    gain_share = shares[TAPS : TAPS + units // 4 // WINDOW].reshape(1, units // 4)
-    return (result[None], kern_share[None], gain_share)
+    return (grads[None], tap_share[None], resp_share)
 
 
 def solution(mesh):

time: 114 us -> 102 us (0.89)
  between operations: 16.5 us -> 0.66 us
  local copies, waits for them, and re-layouts: 3.93 us -> 6.91 us
  Pallas kernels: 92 us -> 94.2 us
  other arithmetic: 1.6 us -> 0 us
    unnamed x12 -> x15, local copies, waits for them, and re-layouts: 0.61 us -> 6.91 us
    pallas_call x1, Pallas kernels: 92 us -> 94.2 us  [on_device(): pl.pallas_call(functools.partial(kernel, sections), out_shape=(jax.ShapeD...]
    slice x1 -> x0, local copies, waits for them, and re-layouts: 1.47 us -> none  [on_device(): arranged = jnp.stack([pick(local_x, order[j]) for j in range(micro)])]
    dynamic_slice x3 -> x0, local copies, waits for them, and re-layouts: 1.19 us -> none  [the longest x2 1.11 us: pick(): return lax.dynamic_index_in_dim(value, index, 0, keepdims=False)]
where the time goes in v2:
time: 102 us
  Pallas kernels  94.2 us (92%)
  local copies, waits for them, and re-layouts  6.91 us (7%)
    pallas_call x1, Pallas kernels, on_device(): pl.pallas_call(functools.partial(kernel, sections), out_shape=(jax.ShapeD...  94.2 us
    unnamed x15, local copies, waits for them, and re-layouts  6.91 us

profile of v2, /device:TPU:0, one launch (start us, length us, event | category | flops | bytes accessed | tf_op | source)
XLA Modules:
  0.0 101.8 jit_solution(6929385137689882935)
XLA Ops:
  0.6 0.0 copy-start
  0.6 1.0 copy-done
  1.6 0.0 copy-start.1
  1.6 1.0 copy-done.1
  2.6 0.0 copy-start.2
  2.6 0.9 copy-done.2
  3.5 0.0 copy-start.3
  3.5 0.7 copy-done.3
  4.2 0.0 copy-start.4
  4.2 0.7 copy-done.4
  4.9 0.0 copy-start.5
  4.9 0.7 copy-done.5
  5.6 94.2 %shard_map.103 = (bf16[4,64,768]{2,1,0:T(8,128)(2,1)S(1)}, f32[49,192]{1,0:T(8,128)S(1)}, f32[1,768]{1,0:T(1,128)S(1)}) custom-call(s32[1,4]{1,0:T(1,128)S(1)} %copy-done.5, bf16[4,64,768]{2,1,0:T(8,128)(2,1)S(1)} %bitcast.7, bf16[49,768]{1,0:T(8,128)(2,1)S(1)} %bitcast.8, bf16[1,768]{1,0:T(2,128)(2,1)S(1)} %copy-done.4, bf16[192,3072]{1,0:T(8,128)(2,1)} %bitcast.10, ...), custom_call_target="tpu_custom_call" | custom-call | tf_op jit(solution)/shard_map/pallas_call | solution.py:447
  99.8 0.7 copy.11
  100.4 0.7 copy.14
  101.2 0.6 copy.15
Async XLA Ops:
  0.6 1.0 copy-start
  1.6 1.0 copy-start.1
  2.6 0.9 copy-start.2
  3.5 0.7 copy-start.3
  4.2 0.7 copy-start.4
  4.9 0.7 copy-start.5

commit v3 on v2

--- a/solution.py
+++ b/solution.py
@@ -19,9 +19,8 @@
 inverse_root_tau = 0.3989422804014327
 
 MESH = pl.DeviceIdType.MESH
-CHUNKS = 6
+CHUNKS = 3
 F_BLOCK = 512
-NT = (((1,), (1,)), ((), ()))
 
 
 def shifted(value, by):
@@ -40,19 +39,26 @@
 def kernel(
     sections,
     plan_ref,
+    x_any,
+    tap_any,
+    gain_any,
+    expand_ref,
+    shrink_ref,
+    resp_any,
+    loss_any,
+    out_ref,
+    tap_out,
+    resp_out,
     x_ref,
     tap_ref,
     gain_ref,
-    expand_ref,
-    shrink_ref,
     resp_ref,
     loss_ref,
-    out_ref,
-    tap_out,
-    resp_out,
     grad_ref,
     ew,
     sw,
+    ewt,
+    swt,
     taps,
     mixed,
     normed,
@@ -71,6 +77,7 @@
     inbox,
     stage,
     landed,
+    fetch_sem,
     local_sem,
     x_send,
     x_recv,
@@ -99,6 +106,21 @@
     beside = 2 * high + (1 - low)
     other = 2 * (1 - high) + (1 - low)
 
+    fetches = [
+        pltpu.make_async_copy(src, dst, fetch_sem.at[k])
+        for k, (src, dst) in enumerate(
+            (
+                (x_any, x_ref),
+                (tap_any, tap_ref),
+                (gain_any, gain_ref),
+                (resp_any, resp_ref),
+                (loss_any, loss_ref),
+            )
+        )
+    ]
+    for copy in fetches:
+        copy.start()
+
     barrier = pltpu.get_barrier_semaphore()
 
     def greet(g, p, d):
@@ -197,6 +219,8 @@
         y_copy(c, 1 - grp).wait_recv()
         h_copy(c, across).start()
 
+    for copy in fetches:
+        copy.wait()
     taps[...] = tap_ref[...].astype(jnp.float32)
     gain = gain_ref[...].astype(jnp.float32)
 
@@ -247,6 +271,7 @@
         cols = pl.ds(pl.multiple_of(b * F_BLOCK, F_BLOCK), F_BLOCK)
         result = jnp.dot(scaled[...], ew[:, cols], preferred_element_type=jnp.float32)
         hid[:, :, cols] = result.reshape(micro, pix, F_BLOCK)
+        ewt[cols, :] = ew[:, cols].T
         return carry
 
     lax.fori_loop(0, units // F_BLOCK, hidden_block, 0)
@@ -273,12 +298,24 @@
         gelu(slot)
         second_part = passes(second_part, 1)
     passes(second_part, CHUNKS)
+    def turn(owner):
+        def block(b, carry):
+            rows = pl.ds(pl.multiple_of(owner * s_rows + b * WINDOW, WINDOW), WINDOW)
+            swt[:, rows] = sw[rows, :].T
+            return carry
+
+        lax.fori_loop(0, s_rows // WINDOW, block, 0)
+
+    locals_[1].wait()
+    turn(me)
+    own_copy(1, beside).wait_recv()
+    turn(beside)
     pass_y(2 * CHUNKS - 1)
-    locals_[1].wait()
-    own_copy(1, beside).wait_recv()
+    turn(across)
     for c in range(CHUNKS, 2 * CHUNKS):
         f_copy(c, other).wait_recv()
         h_copy(c, other).wait_recv()
+    turn(other)
 
     width = channels // PIECES
 
@@ -303,7 +340,7 @@
         weight = jnp.zeros((1, 1), jnp.float32)
         for b in range(units // F_BLOCK):
             cols = slice(b * F_BLOCK, (b + 1) * F_BLOCK)
-            br = lax.dot_general(up, sw[cols, :], NT, preferred_element_type=jnp.float32)
+            br = jnp.dot(up, swt[:, cols], preferred_element_type=jnp.float32)
             back[:, cols] = br
             s = jnp.sum(br * act[slot, :, cols], axis=0, keepdims=True)
             resp_acc[:, cols] += s * ratio[slot, :, cols]
@@ -321,9 +358,7 @@
         bs = jnp.zeros((pix, channels), jnp.float32)
         for b in range(units // F_BLOCK):
             cols = slice(b * F_BLOCK, (b + 1) * F_BLOCK)
-            bs += lax.dot_general(
-                back_hid[:, cols], ew[:, cols], NT, preferred_element_type=jnp.float32
-            )
+            bs += jnp.dot(back_hid[:, cols], ewt[cols, :], preferred_element_type=jnp.float32)
         q = bs * gain
         unit = normed[slot]
         mixed[...] = (
@@ -451,12 +486,19 @@
             jax.ShapeDtypeStruct((TAPS, share), f32),
             jax.ShapeDtypeStruct((1, units // 4), f32),
         ),
-        in_specs=[smem, vmem, vmem, vmem, anywhere, anywhere, vmem, vmem],
+        in_specs=[smem] + [anywhere] * 7,
         out_specs=(vmem, vmem, vmem),
         scratch_shapes=[
             pltpu.VMEM((micro, pix, channels), bf16),
+            pltpu.VMEM((TAPS, channels), bf16),
+            pltpu.VMEM((1, channels), bf16),
+            pltpu.VMEM((1, units), bf16),
+            pltpu.VMEM((micro, pix, channels), bf16),
+            pltpu.VMEM((micro, pix, channels), bf16),
             pltpu.VMEM((channels, units), bf16),
             pltpu.VMEM((units, channels), bf16),
+            pltpu.VMEM((units, channels), bf16),
+            pltpu.VMEM((channels, units), bf16),
             pltpu.VMEM((TAPS, channels), f32),
             pltpu.VMEM((pix, channels), f32),
             pltpu.VMEM((micro, pix, channels), f32),
@@ -475,6 +517,7 @@
             pltpu.VMEM((micro, pix, channels), bf16),
             pltpu.VMEM((4, 64, WINDOW), bf16),
             pltpu.VMEM((3, 64, WINDOW), bf16),
+            dma((5,)),
             dma((2,)),
             dma((2 * CHUNKS,)),
             dma((2 * CHUNKS,)),

time: 102 us -> 88.9 us (0.87)
  Pallas kernels: 94.2 us -> 81 us
    pallas_call x1, Pallas kernels: 94.2 us -> 81 us  [on_device(): pl.pallas_call(functools.partial(kernel, sections), out_shape=(jax.ShapeD...]
where the time goes in v3:
time: 88.9 us; the launch traced here: 88.5 us
  Pallas kernels  81 us (91%)
  local copies, waits for them, and re-layouts  6.91 us (8%)
    pallas_call x1, Pallas kernels, on_device(): pl.pallas_call(functools.partial(kernel, sections), out_shape=(jax.ShapeD...  81 us
    unnamed x15, local copies, waits for them, and re-layouts  6.91 us

profile of v3, /device:TPU:0, one launch (start us, length us, event | category | flops | bytes accessed | tf_op | source)
XLA Modules:
  0.0 88.5 jit_solution(2884010852412868133)
XLA Ops:
  0.6 0.0 copy-start
  0.6 1.0 %copy-done = bf16[1,4,64,768]{3,2,1,0:T(8,128)(2,1)S(1)} copy-done((bf16[1,4,64,768]{3,2,1,0:T(8,128)(2,1)S(1)}, bf16[1,4,64,768]{3,2,1,0:T(8,128)(2,1)}, u32[]{:S(2)}) %copy-start) | copy-done | bytes 393240
  1.6 0.0 copy-start.1
  1.6 1.0 %copy-done.1 = bf16[4,64,768]{2,1,0:T(8,128)(2,1)S(1)} copy-done((bf16[4,64,768]{2,1,0:T(8,128)(2,1)S(1)}, bf16[4,64,768]{2,1,0:T(8,128)(2,1)}, u32[]{:S(2)}) %copy-start.1) | copy-done | bytes 393240
  2.6 0.0 copy-start.2
  2.6 0.9 %copy-done.2 = bf16[1,49,768]{2,1,0:T(8,128)(2,1)S(1)} copy-done((bf16[1,49,768]{2,1,0:T(8,128)(2,1)S(1)}, bf16[1,49,768]{2,1,0:T(8,128)(2,1)}, u32[]{:S(2)}) %copy-start.2) | copy-done | bytes 75288
  3.5 0.0 copy-start.3
  3.5 0.7 copy-done.3
  4.2 0.0 copy-start.4
  4.2 0.7 copy-done.4
  4.9 0.0 copy-start.5
  4.9 0.7 copy-done.5
  5.6 81.0 %shard_map.103 = (bf16[4,64,768]{2,1,0:T(8,128)(2,1)S(1)}, f32[49,192]{1,0:T(8,128)S(1)}, f32[1,768]{1,0:T(1,128)S(1)}) custom-call(s32[1,4]{1,0:T(1,128)S(1)} %copy-done.5, bf16[4,64,768]{2,1,0:T(8,128)(2,1)S(1)} %bitcast.7, bf16[49,768]{1,0:T(8,128)(2,1)S(1)} %bitcast.8, bf16[1,768]{1,0:T(2,128)(2,1)S(1)} %copy-done.4, bf16[192,3072]{1,0:T(8,128)(2,1)} %bitcast.10, ...), custom_call_target="tpu_custom_call" | custom-call | tf_op jit(solution)/shard_map/pallas_call | solution.py:482
  86.5 0.7 copy.11
  87.2 0.7 copy.14
  88.0 0.6 copy.15
Async XLA Ops:
  0.6 1.0 %copy-start = (bf16[1,4,64,768]{3,2,1,0:T(8,128)(2,1)S(1)}, bf16[1,4,64,768]{3,2,1,0:T(8,128)(2,1)}, u32[]{:S(2)}) copy-start(bf16[1,4,64,768]{3,2,1,0:T(8,128)(2,1)} %param.8) | copy-start | bytes 1179652
  1.6 1.0 %copy-start.1 = (bf16[4,64,768]{2,1,0:T(8,128)(2,1)S(1)}, bf16[4,64,768]{2,1,0:T(8,128)(2,1)}, u32[]{:S(2)}) copy-start(bf16[4,64,768]{2,1,0:T(8,128)(2,1)} %loss_any.1) | copy-start | bytes 1179652
  2.6 0.9 %copy-start.2 = (bf16[1,49,768]{2,1,0:T(8,128)(2,1)S(1)}, bf16[1,49,768]{2,1,0:T(8,128)(2,1)}, u32[]{:S(2)}) copy-start(bf16[1,49,768]{2,1,0:T(8,128)(2,1)} %param.9) | copy-start | bytes 225796
  3.5 0.7 copy-start.3
  4.2 0.7 copy-start.4
  4.9 0.7 copy-start.5

commit v4 on v3

--- a/solution.py
+++ b/solution.py
@@ -535,7 +535,7 @@
             dma((3,)),
         ],
         compiler_params=pltpu.CompilerParams(
-            collective_id=0, has_side_effects=True, vmem_limit_bytes=52 * 1024 * 1024
+            collective_id=0, has_side_effects=True, vmem_limit_bytes=62 * 1024 * 1024
         ),
     )(
         plan,

time: 88.9 us -> 86.8 us (0.976)
  local copies, waits for them, and re-layouts: 6.91 us -> 4.52 us
    unnamed x15 -> x3, local copies, waits for them, and re-layouts: 6.91 us -> 4.52 us
where the time goes in v4:
time: 86.8 us; the launch traced here: 86.5 us
  Pallas kernels  81.4 us (94%)
  local copies, waits for them, and re-layouts  4.52 us (5%)
    pallas_call x1, Pallas kernels, on_device(): pl.pallas_call(functools.partial(kernel, sections), out_shape=(jax.ShapeD...  81.4 us
    unnamed x3, local copies, waits for them, and re-layouts  4.52 us

profile of v4, /device:TPU:0, one launch (start us, length us, event | category | flops | bytes accessed | tf_op | source)
XLA Modules:
  0.0 86.5 jit_solution(13911733797607206909)
XLA Ops:
  0.6 81.4 %shard_map.103 = (bf16[4,64,768]{2,1,0:T(8,128)(2,1)}, f32[49,192]{1,0:T(8,128)}, f32[1,768]{1,0:T(1,128)}) custom-call(s32[1,4]{1,0:T(1,128)} %plan_ref.1, bf16[4,64,768]{2,1,0:T(8,128)(2,1)} %bitcast.9, bf16[49,768]{1,0:T(8,128)(2,1)} %bitcast.10, bf16[1,768]{1,0:T(2,128)(2,1)} %gain_any.1, bf16[192,3072]{1,0:T(8,128)(2,1)} %bitcast.6, ...), custom_call_target="tpu_custom_call" | custom-call | tf_op jit(solution)/shard_map/pallas_call | solution.py:482
  82.0 1.5 %copy.11 = f32[1,49,192]{2,0,1:T(1,128)} copy(f32[1,49,192]{2,1,0:T(8,128)} %bitcast.11) | data formatting | bytes 75264
  83.5 1.8 %copy.14 = bf16[1,4,64,768]{3,2,1,0:T(8,128)(2,1)} copy(bf16[1,4,64,768]{3,2,1,0:T(8,128)(2,1)} %bitcast.8) | data formatting | bytes 786432
  85.3 1.3 %copy.15 = f32[1,768]{1,0:T(1,128)} copy(f32[1,768]{1,0:T(1,128)} %get-tuple-element.17) | data formatting | bytes 6144
